TPU v7x, 32 devices: a whole 2x2x4 slice. The times are simulated.
32 devices in a mesh: seq: 16 (over z, y, x), tp: 2 (over core).
Axes of the slice: x: 2, y: 2, z: 4, core: 2. Of those that a mesh axis runs over, the one named last changes fastest.
Arguments:
- student: bfloat16 [4096, 2048], P('seq'), may hold values from -6 to 6
- projector: bfloat16 [2, 4224, 2048], P('tp', 'seq'), may hold values from -0.125 to 0.125
- teacher: bfloat16 [2, 4096, 8448], P(None, 'seq', 'tp'), may hold values from -6 to 6
- layer_index: int32 [4096], P('seq'), may hold values from 0 to 1
- valid_mask: int32 [4096], P('seq'), may hold values 0 or 1
Outputs:
- grad_student: bfloat16 [4096, 2048], P('seq', 'tp')
- token_loss: float32 [4096], P(('seq', 'tp'))
All inputs are finite; a program needn't handle non-finite values. No bound on the sum of `valid_mask` on one device may be relied on, other than what follows from the above.
Results may differ from a plain program's by a relative error of at most 0.0034.
Values may be sent and summed in bfloat16 or wider, within the bound.
A program may use at most 64 MiB of HBM per device.

v0:
```python
import jax
import jax.numpy as jnp
from jax import lax
from jax.sharding import PartitionSpec as P

HW = 8448


def body(student, projector, teacher, layer_index, valid_mask):
    rows_dev = student.shape[0]
    feat_dim = student.shape[1]
    chosen = teacher[0]
    chosen = jnp.where((layer_index == 1)[:, None], teacher[1], chosen)
    weight = valid_mask.astype(jnp.float32)[:, None]
    gathered = lax.all_gather(projector, "seq", axis=1, tiled=True)
    flat_rows = gathered.reshape(-1, feat_dim)
    predicted = lax.dot_general(
        student, flat_rows, (((1,), (1,)), ((), ())), preferred_element_type=jnp.float32
    )
    difference = predicted - chosen.astype(jnp.float32)
    masked_err = (weight * difference).astype(jnp.bfloat16)
    grad_term = jnp.dot(masked_err, flat_rows, preferred_element_type=jnp.float32)
    squares = jnp.sum(difference * difference, axis=1)
    summed, totals = (
        lax.psum_scatter(grad_term, "tp", scatter_dimension=1, tiled=True),
        lax.psum_scatter(squares, "tp", scatter_dimension=0, tiled=True),
    )
    tp_count = lax.axis_size("tp")
    share_rows = rows_dev // tp_count
    own_mask = lax.dynamic_slice_in_dim(
        valid_mask, lax.axis_index("tp") * share_rows, share_rows
    ).astype(jnp.float32)
    return (summed.astype(jnp.bfloat16), own_mask * totals / HW)


def solution(mesh):
    placed = (P("seq", None), P("tp", "seq", None), P(None, "seq", "tp"), P("seq"), P("seq"))
    return jax.shard_map(
        body,
        mesh=mesh,
        in_specs=placed,
        out_specs=(P("seq", "tp"), P(("seq", "tp"))),
        check_vma=False,
    )
```

profile of v0, /device:TPU:0, one launch (start us, length us, event | category | flops | bytes accessed | tf_op | source)
XLA Modules:
  0.0 260.1 jit_solution(11113816485252569042)
XLA Ops:
  7.2 0.0 copy-start
  7.2 0.0 all-gather.2.cloned.1.call-start
  7.2 0.7 all-gather.2.cloned.1.call-update
  7.9 0.0 reduce-scatter.2.cloned.1.call-start
  8.0 0.7 convert_element_type.15
  8.6 0.7 broadcast_compare_fusion
  9.3 200.8 %all-gather.2.cloned.1.call-done = bf16[1,4224,2048]{2,1,0:T(8,128)(2,1)} async-done(((bf16[1,264,2048]{2,1,0:T(8,128)(2,1)}), bf16[1,4224,2048]{2,1,0:T(8,128)(2,1)}) %all-gather.2.cloned.1.call-update) | async-done | bytes 17301520 | tf_op jit(solution)/shard_map/all_gather | solution.py:15
  210.2 0.0 copy-done
  210.2 19.6 %multiply_reduce_fusion = (f32[256]{0:T(256)S(1)}, f32[256,4224]{1,0:T(8,128)}) fusion(bf16[2,256,4224]{2,1,0:T(8,128)(2,1)} %param.7, pred[256]{0:T(512)(128)(4,1)S(1)} %broadcast_compare_fusion, bf16[256,2048]{1,0:T(8,128)(2,1)S(1)} %copy-done, bf16[1,4224,2048]{2,1,0:T(8,128)(2,1)} %all-gather.2.cloned.1.call-done), kind=kOutput, calls=%fused_computation.5 | convolution fusion | flops 4434591744 | bytes 27002112 | tf_op jit(solution)/shard_map/dot_general | solution.py:17
  229.8 0.0 copy-start.2
  229.8 0.0 copy-start.1
  229.8 13.4 %fusion = f32[256,2048]{1,0:T(8,128)} fusion(bf16[1,4224,2048]{2,1,0:T(8,128)(2,1)} %all-gather.2.cloned.1.call-done, f32[256,4224]{1,0:T(8,128)} %get-tuple-element.3, f32[256]{0:T(256)S(1)} %convert_element_type.15), kind=kOutput, calls=%fused_computation | convolution fusion | flops 4431347712 | bytes 23725056 | tf_op jit(solution)/shard_map/dot_general | solution.py:22
  243.2 0.0 reduce-scatter.2.cloned.1.call-update
  243.2 0.0 copy-done.2
  243.2 0.6 dynamic-slice
  244.5 2.5 all-reduce
  246.9 0.0 copy-done.1
  246.9 0.6 fusion.8
  247.5 3.6 %reduce-scatter.2.cloned.1.call-done = f32[256,1024]{1,0:T(8,128)} async-done(((f32[256,2048]{1,0:T(8,128)}), f32[256,1024]{1,0:T(8,128)}) %reduce-scatter.2.cloned.1.call-update) | async-done | bytes 1048592 | tf_op jit(solution)/shard_map/reduce_scatter | solution.py:25
  251.2 2.1 convert_element_type.18
Async XLA Ops:
  7.2 203.0 %copy-start = (bf16[256,2048]{1,0:T(8,128)(2,1)S(1)}, bf16[256,2048]{1,0:T(8,128)(2,1)}, u32[]{:S(2)}) copy-start(bf16[256,2048]{1,0:T(8,128)(2,1)} %param.5) | copy-start | bytes 3145732
  7.2 203.0 %all-gather.2.cloned.1.call-start = ((), (), s32[]{:S(2)}) async-start(), calls=%async_computation.1 | async-start | bytes 18382848 | tf_op jit(solution)/shard_map/all_gather | solution.py:15
  7.9 243.3 %reduce-scatter.2.cloned.1.call-start = ((), (), s32[]{:S(2)}) async-start(), calls=%async_computation.2 | async-start | bytes 3145728 | tf_op jit(solution)/shard_map/reduce_scatter | solution.py:25
  229.8 13.5 %copy-start.2 = (u32[32]{0:T(128)S(1)}, u32[32]{0:T(128)}, u32[]{:S(2)}) copy-start(u32[32]{0:T(128)} %constant.20) | copy-start | bytes 388
  229.8 17.2 %copy-start.1 = (s32[256]{0:T(256)S(1)}, s32[256]{0:T(256)}, u32[]{:S(2)}) copy-start(s32[256]{0:T(256)} %param.9) | copy-start | bytes 3076
Sparse Core Ops, SparseCore 0:
  10.8 199.3 all-gather.1
  243.3 7.7 reduce-scatter.1
where the time goes:
time: 260 us
  waiting for transfers between devices  205 us (79%)
  matrix products  33 us (13%)
  between operations  14.7 us (6%)
  other arithmetic  4.05 us (2%)
    all_gather x1, waiting for transfers between devices, body(): gathered = lax.all_gather(projector, 'seq', axis=1, tiled=True)  201 us
    dot_general x1, matrix products, body(): lax.dot_general(student, flat_rows, (((1,), (1,)), ((), ())), preferred_e...  19.6 us
    dot_general x1, matrix products, body(): jnp.dot(masked_err, flat_rows, preferred_element_type=jnp.float32)  13.4 us
  transfers between devices with their start and end apart: 2, of which 2 were waited for; matrix products, arithmetic and copies ran while one was open for 1% of the time, Pallas kernels for 0%

commit v1 on v0

v1 whole, which is shorter than its diff:
```python
import jax
import jax.numpy as jnp
from jax import lax
from jax.experimental import pallas as pl
from jax.experimental.pallas import tpu as pltpu
from jax.sharding import PartitionSpec as P

MESH = pl.DeviceIdType.MESH
LINE, PLANE, CORES = 4, 4, 2


def plain_body(student, projector, teacher, layer_index, valid_mask):
    rows_dev, feat_dim = student.shape
    chosen = jnp.where((layer_index == 1)[:, None], teacher[1], teacher[0])
    weight = valid_mask.astype(jnp.float32)[:, None]
    gathered = lax.all_gather(projector, "seq", axis=1, tiled=True)
    flat_rows = gathered.reshape(-1, feat_dim)
    predicted = lax.dot_general(
        student, flat_rows, (((1,), (1,)), ((), ())), preferred_element_type=jnp.float32
    )
    difference = predicted - chosen.astype(jnp.float32)
    masked_err = (weight * difference).astype(jnp.bfloat16)
    grad_term = jnp.dot(masked_err, flat_rows, preferred_element_type=jnp.float32)
    squares = jnp.sum(difference * difference, axis=1)
    summed = lax.psum_scatter(grad_term, "tp", scatter_dimension=1, tiled=True)
    totals = lax.psum_scatter(squares, "tp", scatter_dimension=0, tiled=True)
    tp_count = lax.axis_size("tp")
    share_rows = rows_dev // tp_count
    own_mask = lax.dynamic_slice_in_dim(
        valid_mask, lax.axis_index("tp") * share_rows, share_rows
    ).astype(jnp.float32)
    return (summed.astype(jnp.bfloat16), own_mask * totals / (teacher.shape[2] * tp_count))


def kernel(
    student, projector, teacher, layer, mask, grad_out, loss_out,
    held, states, layers, stage, chosen, total, squares, give, take, give_sq, take_sq, done, crossed,
    arrived, up_sem, down_sem, over_sem, own_sem,
    state_send, state_recv, load_sem, ch_send, ch_recv, g_send, g_recv, q_send, q_recv, x_send, x_recv,
):
    feat_dim = student.shape[1]
    half = feat_dim // 2
    rows = projector.shape[1]
    tok = student.shape[0]
    share = tok // CORES
    width = teacher.shape[2] * CORES
    seq, core = lax.axis_index("seq"), lax.axis_index("tp")
    z, q = seq // PLANE, seq % PLANE
    y, x = q // 2, q % 2
    other = 1 - core

    def across(r):
        return (1 - y if r // 2 else y) * 2 + (1 - x if r % 2 else x)

    def device(r, k):
        return (z * PLANE + across(r), k)

    sibling = (seq, other)
    above, below = (seq + PLANE, core), (seq - PLANE, core)

    loads = [pltpu.make_async_copy(teacher, layers, load_sem.at[0])]
    loads[0].start()
    own_state = pltpu.make_async_copy(
        student.at[pl.ds(core * share, share), :], states.at[pl.ds(0, share), :], load_sem.at[1])
    own_state.start()
    own_rows = [
        pltpu.make_async_copy(
            projector.at[0, :, pl.ds(h * half, half)], held.at[h, z, core], own_sem.at[h])
        for h in range(2)
    ]
    for copy in own_rows:
        copy.start()

    barrier = pltpu.get_barrier_semaphore()
    peers = [sibling] + [device(r, k) for r in range(1, PLANE) for k in range(CORES)]
    for peer in peers:
        pl.semaphore_signal(barrier, inc=1, device_id=peer, device_id_type=MESH)

    @pl.when(z > 0)
    def _():
        pl.semaphore_signal(barrier, inc=1, device_id=below, device_id_type=MESH)

    @pl.when(z < LINE - 1)
    def _():
        pl.semaphore_signal(barrier, inc=1, device_id=above, device_id_type=MESH)

    pl.semaphore_wait(barrier, len(peers) + jnp.where(z > 0, 1, 0) + jnp.where(z < LINE - 1, 1, 0))

    def rows_copy(source, h, zs, sem, target):
        return pltpu.make_async_remote_copy(
            src_ref=source, dst_ref=held.at[h, zs, core], send_sem=sem.at[h, zs],
            recv_sem=arrived.at[h, zs, core], device_id=target, device_id_type=MESH)

    def pass_on(source, h, zs, act):
        @pl.when((z < LINE - 1) & (zs <= z))
        def _():
            act(rows_copy(source, h, zs, up_sem, above))

        @pl.when((z > 0) & (zs >= z))
        def _():
            act(rows_copy(source, h, zs, down_sem, below))

        act(rows_copy(source, h, zs, over_sem, sibling))

    def landed(h, zs, k):
        pltpu.make_async_remote_copy(
            src_ref=held.at[h, zs, k], dst_ref=held.at[h, zs, k], send_sem=over_sem.at[h, zs],
            recv_sem=arrived.at[h, zs, k], device_id=sibling, device_id_type=MESH).wait_recv()

    for h in range(2):
        pass_on(projector.at[0, :, pl.ds(h * half, half)], h, z, lambda copy: copy.start())

    state_copies = [
        pltpu.make_async_remote_copy(
            src_ref=student.at[pl.ds(core * share, share), :],
            dst_ref=states.at[pl.ds(r * share, share), :],
            send_sem=state_send.at[r], recv_sem=state_recv.at[r],
            device_id=device(r, core), device_id_type=MESH)
        for r in range(1, PLANE)
    ]
    for copy in state_copies:
        copy.start()

    loads[0].wait()
    step_rows = 32

    def choose(i, carry):
        at = pl.multiple_of(i * step_rows, step_rows)
        second = layer[pl.ds(at, step_rows), :] == 1
        for target in range(PLANE):
            for zs in range(LINE):
                first_column = (zs * PLANE + target) * rows
                base = first_column // 128 * 128
                shift = first_column - base
                span = -(-(shift + rows) // 128) * 128
                a = layers[0, pl.ds(at, step_rows), base:base + span].astype(jnp.float32)
                b = layers[1, pl.ds(at, step_rows), base:base + span].astype(jnp.float32)
                picked = jnp.where(second, b, a)
                if shift:
                    picked = pltpu.roll(picked, span - shift, 1)
                stage[target, zs, pl.ds(at, step_rows), :] = picked[:, :rows].astype(jnp.bfloat16)
        return carry

    lax.fori_loop(0, tok // step_rows, choose, 0)

    def chosen_copy(r, k):
        return pltpu.make_async_remote_copy(
            src_ref=stage.at[across(r), :, pl.ds(k * share, share), :],
            dst_ref=chosen.at[core, :, pl.ds(r * share, share), :],
            send_sem=ch_send.at[r, k], recv_sem=ch_recv.at[r, core],
            device_id=device(r, k), device_id_type=MESH)

    own_chosen = pltpu.make_async_copy(
        stage.at[q, :, pl.ds(core * share, share), :],
        chosen.at[core, :, pl.ds(0, share), :], load_sem.at[2])
    own_chosen.start()
    to_sibling = chosen_copy(0, other)
    to_sibling.start()
    chosen_copies = [chosen_copy(r, k) for r in range(1, PLANE) for k in range(CORES)]
    for copy in chosen_copies:
        copy.start()

    total[...] = jnp.zeros_like(total)
    squares[...] = jnp.zeros_like(squares)

    def arrive(distance):
        for h in range(2):
            for sign in (-1, 1):
                zs = z + sign * distance

                @pl.when((zs >= 0) & (zs < LINE))
                def _():
                    landed(h, zs, core)
                    pass_on(held.at[h, zs, core], h, zs, lambda copy: copy.start())

    arrive(1)
    arrive(2)
    for copy in own_rows:
        copy.wait()
    own_state.wait()
    own_chosen.wait()
    for copy in state_copies:
        copy.wait_recv()
    for r in range(PLANE):
        for k in range(CORES):
            if r == 0:
                continue
            pltpu.make_async_remote_copy(
                src_ref=chosen.at[k, :, pl.ds(r * share, share), :],
                dst_ref=chosen.at[k, :, pl.ds(r * share, share), :],
                send_sem=ch_send.at[r, k], recv_sem=ch_recv.at[r, k],
                device_id=sibling, device_id_type=MESH).wait_recv()
    pltpu.make_async_remote_copy(
        src_ref=chosen.at[other, :, pl.ds(0, share), :],
        dst_ref=chosen.at[other, :, pl.ds(0, share), :],
        send_sem=ch_send.at[0, other], recv_sem=ch_recv.at[0, other],
        device_id=sibling, device_id_type=MESH).wait_recv()

    def work(zs):
        for h in range(2):
            landed(h, zs, other)

        def one(k, carry):
            predicted = sum(
                lax.dot_general(
                    states[:, h * half:(h + 1) * half], held[h, zs, k],
                    (((1,), (1,)), ((), ())), preferred_element_type=jnp.float32)
                for h in range(2))
            difference = predicted - chosen[k, zs].astype(jnp.float32)
            squares[...] += jnp.sum(difference * difference, axis=1, keepdims=True)
            err = difference.astype(jnp.bfloat16)
            for h in range(2):
                total[:, h * half:(h + 1) * half] += jnp.dot(
                    err, held[h, zs, k], preferred_element_type=jnp.float32)
            return carry

        lax.fori_loop(0, CORES, one, 0)

    def round_of(distance, carry):
        @pl.when(distance == LINE - 1)
        def _():
            arrive(LINE - 1)

        @pl.when(z - distance >= 0)
        def _():
            work(z - distance)

        @pl.when((distance > 0) & (z + distance < LINE))
        def _():
            work(z + distance)

        return carry

    lax.fori_loop(0, LINE, round_of, 0)

    def square_row(r):
        column = jnp.broadcast_to(squares[r * share:(r + 1) * share, :], (share, 128))
        return column.T[:8, :]

    sums = []
    for r in (3, 1, 2):
        give[r - 1] = total[r * share:(r + 1) * share, :].astype(jnp.bfloat16)
        copy = pltpu.make_async_remote_copy(
            src_ref=give.at[r - 1], dst_ref=take.at[r - 1],
            send_sem=g_send.at[r - 1], recv_sem=g_recv.at[r - 1],
            device_id=device(r, core), device_id_type=MESH)
        copy.start()
        give_sq[r - 1] = square_row(r)
        copy_sq = pltpu.make_async_remote_copy(
            src_ref=give_sq.at[r - 1], dst_ref=take_sq.at[r - 1],
            send_sem=q_send.at[r - 1], recv_sem=q_recv.at[r - 1],
            device_id=device(r, core), device_id_type=MESH)
        copy_sq.start()
        sums += [copy, copy_sq]
    for copy in sums:
        copy.wait_recv()

    own_weight = mask[pl.ds(pl.multiple_of(core * share, share), share), :].astype(jnp.float32)
    for h in range(2):
        at = slice(h * half, (h + 1) * half)
        summed = total[:share, at]
        for r in range(1, PLANE):
            summed += take[r - 1, :, at].astype(jnp.float32)
        done[h] = (own_weight * summed).astype(jnp.bfloat16)
    cross = pltpu.make_async_remote_copy(
        src_ref=done.at[other], dst_ref=crossed, send_sem=x_send, recv_sem=x_recv,
        device_id=sibling, device_id_type=MESH)
    cross.start()
    grad_out[pl.ds(pl.multiple_of(core * share, share), share), :] = done[core]
    all_squares = square_row(0) + take_sq[0] + take_sq[1] + take_sq[2]
    weight_row = jnp.broadcast_to(own_weight, (share, 128)).T[:8, :]
    loss_out[...] = (weight_row * all_squares / width)[:1, :]
    cross.wait_recv()
    grad_out[pl.ds(pl.multiple_of(other * share, share), share), :] = crossed[...]

    cross.wait_send()
    for copy in sums + state_copies + chosen_copies + [to_sibling]:
        copy.wait_send()

    def sent(zs, carry):
        for h in range(2):
            pass_on(held.at[h, zs, core], h, zs, lambda copy: copy.wait_send())
        return carry

    lax.fori_loop(0, LINE, sent, 0)


def fast_body(student, projector, teacher, layer_index, valid_mask):
    tok, feat_dim = student.shape
    rows = projector.shape[1]
    half, share = feat_dim // 2, tok // CORES
    bf16, f32 = jnp.bfloat16, jnp.float32
    dma = pltpu.SemaphoreType.DMA
    flops = 4 * tok * CORES * rows * LINE * CORES * feat_dim
    grad, loss = pl.pallas_call(
        kernel,
        out_shape=(
            jax.ShapeDtypeStruct((tok, half), bf16),
            jax.ShapeDtypeStruct((1, share), f32),
        ),
        in_specs=[pl.BlockSpec(memory_space=pl.ANY)] * 3
        + [pl.BlockSpec(memory_space=pltpu.VMEM)] * 2,
        out_specs=(pl.BlockSpec(memory_space=pltpu.VMEM),) * 2,
        scratch_shapes=[
            pltpu.VMEM((2, LINE, CORES, rows, half), bf16),
            pltpu.VMEM((PLANE * share, feat_dim), bf16),
            pltpu.VMEM(teacher.shape, bf16),
            pltpu.VMEM((PLANE, LINE, tok, rows), bf16),
            pltpu.VMEM((CORES, LINE, PLANE * share, rows), bf16),
            pltpu.VMEM((PLANE * share, feat_dim), f32),
            pltpu.VMEM((PLANE * share, 1), f32),
            pltpu.VMEM((PLANE - 1, share, feat_dim), bf16),
            pltpu.VMEM((PLANE - 1, share, feat_dim), bf16),
            pltpu.VMEM((PLANE - 1, 8, share), f32),
            pltpu.VMEM((PLANE - 1, 8, share), f32),
            pltpu.VMEM((2, share, half), bf16),
            pltpu.VMEM((share, half), bf16),
            dma((2, LINE, CORES)), dma((2, LINE)), dma((2, LINE)), dma((2, LINE)), dma((2,)),
            dma((PLANE,)), dma((PLANE,)), dma((3,)), dma((PLANE, CORES)), dma((PLANE, CORES)),
            dma((PLANE - 1,)), dma((PLANE - 1,)), dma((PLANE - 1,)), dma((PLANE - 1,)),
            dma(()), dma(()),
        ],
        compiler_params=pltpu.CompilerParams(
            collective_id=0, has_side_effects=True, vmem_limit_bytes=48 * 1024 * 1024),
        cost_estimate=pl.CostEstimate(flops=flops, bytes_accessed=16 * 1024 * 1024, transcendentals=0),
    )(student, projector, teacher, layer_index[:, None], valid_mask[:, None])
    return grad, loss.reshape(share)


def solution(mesh):
    placed = (P("seq", None), P("tp", "seq", None), P(None, "seq", "tp"), P("seq"), P("seq"))
    body = fast_body if dict(mesh.shape) == {"seq": LINE * PLANE, "tp": CORES} else plain_body
    return jax.shard_map(
        body,
        mesh=mesh,
        in_specs=placed,
        out_specs=(P("seq", "tp"), P(("seq", "tp"))),
        check_vma=False,
    )
```

time: 260 us -> 116 us (0.45)
  waiting for transfers between devices: 205 us -> 0 us
  Pallas kernels: 0 us -> 109 us
  matrix products: 33 us -> 0 us
  between operations: 14.7 us -> 0.66 us
  local copies, waits for them, and re-layouts: 0.6 us -> 5.38 us
  other arithmetic: 4.05 us -> 0 us
    all_gather x1 -> x0, waiting for transfers between devices: 201 us -> none  [body(): gathered = lax.all_gather(projector, 'seq', axis=1, tiled=True)]
    pallas_call x0 -> x1, Pallas kernels: none -> 109 us  [fast_body(): pl.pallas_call(kernel, out_shape=(jax.ShapeDtypeStruct((tok, half), bf16)...]
    dot_general x2 -> x0, matrix products: 33 us -> none  [the longest x1 19.6 us: body(): lax.dot_general(student, flat_rows, (((1,), (1,)), ((), ())), preferred_e...]
    reduce_scatter x1 -> x0, waiting for transfers between devices: 3.64 us -> none  [body(): lax.psum_scatter(grad_term, 'tp', scatter_dimension=1, tiled=True)]
    unnamed x7 -> x6, local copies, waits for them, and re-layouts: 0.6 us -> 3.77 us
    convert_element_type x2 -> x0, other arithmetic: 2.78 us -> none  [the longest x1 2.09 us: body(): return (summed.astype(jnp.bfloat16), own_mask * totals / HW)]
  transfers between devices with their start and end apart: 2 -> 0, of which waited for: 2 -> 0; matrix products, arithmetic and copies ran while one was open for 1% -> 0% of each run, Pallas kernels for 0% -> 0%
where the time goes in v1:
time: 116 us; the launch traced here: 115 us
  Pallas kernels  109 us (94%)
  local copies, waits for them, and re-layouts  5.38 us (5%)
    pallas_call x1, Pallas kernels, fast_body(): pl.pallas_call(kernel, out_shape=(jax.ShapeDtypeStruct((tok, half), bf16)...  109 us
    unnamed x6, local copies, waits for them, and re-layouts  3.77 us

profile of v1, /device:TPU:0, one launch (start us, length us, event | category | flops | bytes accessed | tf_op | source)
XLA Modules:
  0.0 115.5 jit_solution(11725692990604101920)
XLA Ops:
  0.6 0.8 copy.7.layer
  1.4 0.8 copy.8.mask
  2.3 0.0 copy-start
  2.3 1.2 %copy-done = bf16[1,264,2048]{2,1,0:T(8,128)(2,1)S(1)} copy-done((bf16[1,264,2048]{2,1,0:T(8,128)(2,1)S(1)}, bf16[1,264,2048]{2,1,0:T(8,128)(2,1)}, u32[]{:S(2)}) %copy-start) | copy-done | bytes 1081368
  3.5 0.0 copy-start.1
  3.5 1.2 %copy-done.1 = bf16[256,2048]{1,0:T(8,128)(2,1)S(1)} copy-done((bf16[256,2048]{1,0:T(8,128)(2,1)S(1)}, bf16[256,2048]{1,0:T(8,128)(2,1)}, u32[]{:S(2)}) %copy-start.1) | copy-done | bytes 1048600
  4.7 109.4 %shard_map.68 = (bf16[256,1024]{1,0:T(8,128)(2,1)S(1)}, f32[1,128]{1,0:T(1,128)S(1)}) custom-call(bf16[256,2048]{1,0:T(8,128)(2,1)S(1)} %copy-done.1, bf16[1,264,2048]{2,1,0:T(8,128)(2,1)S(1)} %copy-done, bf16[2,256,4224]{2,1,0:T(8,128)(2,1)} %teacher.1, s32[256,1]{1,0:T(8,128)S(1)} %copy.7.layer, s32[256,1]{1,0:T(8,128)S(1)} %copy.8.mask), custom_call_target="tpu_custom_call" | custom-call | flops 8858370048 | bytes 16777216 | tf_op jit(solution)/shard_map/pallas_call | solution.py:295
  114.2 0.8 copy.11
  115.0 0.5 copy.12
Async XLA Ops:
  2.3 1.2 %copy-start = (bf16[1,264,2048]{2,1,0:T(8,128)(2,1)S(1)}, bf16[1,264,2048]{2,1,0:T(8,128)(2,1)}, u32[]{:S(2)}) copy-start(bf16[1,264,2048]{2,1,0:T(8,128)(2,1)} %projector.1) | copy-start | bytes 3244036
  3.5 1.2 %copy-start.1 = (bf16[256,2048]{1,0:T(8,128)(2,1)S(1)}, bf16[256,2048]{1,0:T(8,128)(2,1)}, u32[]{:S(2)}) copy-start(bf16[256,2048]{1,0:T(8,128)(2,1)} %student.1) | copy-start | bytes 3145732

commit v2 on v1

--- a/solution.py
+++ b/solution.py
@@ -6,6 +6,7 @@
 from jax.sharding import PartitionSpec as P
 
 MESH = pl.DeviceIdType.MESH
+PLACE = {0: 0, 2: 1, 3: 2, 1: 3}
 LINE, PLANE, CORES = 4, 4, 2
 
 
@@ -34,9 +35,9 @@
 
 def kernel(
     student, projector, teacher, layer, mask, grad_out, loss_out,
-    held, states, layers, stage, chosen, total, squares, give, take, give_sq, take_sq, done, crossed,
+    held, states, layers, second, stage, chosen, total, squares, errors, give, take, give_mid, take_mid, give_sq, take_sq, done, crossed,
     arrived, up_sem, down_sem, over_sem, own_sem,
-    state_send, state_recv, load_sem, ch_send, ch_recv, g_send, g_recv, q_send, q_recv, x_send, x_recv,
+    state_send, state_recv, load_sem, ch_send, ch_recv, g_send, g_recv, m_send, m_recv, q_send, q_recv, x_send, x_recv,
 ):
     feat_dim = student.shape[1]
     half = feat_dim // 2
@@ -113,7 +114,7 @@
     state_copies = [
         pltpu.make_async_remote_copy(
             src_ref=student.at[pl.ds(core * share, share), :],
-            dst_ref=states.at[pl.ds(r * share, share), :],
+            dst_ref=states.at[pl.ds(PLACE[r] * share, share), :],
             send_sem=state_send.at[r], recv_sem=state_recv.at[r],
             device_id=device(r, core), device_id_type=MESH)
         for r in range(1, PLANE)
@@ -123,10 +124,12 @@
 
     loads[0].wait()
     step_rows = 32
+    for k in range(CORES):
+        second[k * share:(k + 1) * share, :] = jnp.broadcast_to(layer[k:k + 1, :], (share, share)).T
 
     def choose(i, carry):
         at = pl.multiple_of(i * step_rows, step_rows)
-        second = layer[pl.ds(at, step_rows), :] == 1
+        mapped = second[pl.ds(at, step_rows), :1] == 1
         for target in range(PLANE):
             for zs in range(LINE):
                 first_column = (zs * PLANE + target) * rows
@@ -135,7 +138,7 @@
                 span = -(-(shift + rows) // 128) * 128
                 a = layers[0, pl.ds(at, step_rows), base:base + span].astype(jnp.float32)
                 b = layers[1, pl.ds(at, step_rows), base:base + span].astype(jnp.float32)
-                picked = jnp.where(second, b, a)
+                picked = jnp.where(mapped, b, a)
                 if shift:
                     picked = pltpu.roll(picked, span - shift, 1)
                 stage[target, zs, pl.ds(at, step_rows), :] = picked[:, :rows].astype(jnp.bfloat16)
@@ -146,7 +149,7 @@
     def chosen_copy(r, k):
         return pltpu.make_async_remote_copy(
             src_ref=stage.at[across(r), :, pl.ds(k * share, share), :],
-            dst_ref=chosen.at[core, :, pl.ds(r * share, share), :],
+            dst_ref=chosen.at[core, :, pl.ds(PLACE[r] * share, share), :],
             send_sem=ch_send.at[r, k], recv_sem=ch_recv.at[r, core],
             device_id=device(r, k), device_id_type=MESH)
 
@@ -186,8 +189,8 @@
             if r == 0:
                 continue
             pltpu.make_async_remote_copy(
-                src_ref=chosen.at[k, :, pl.ds(r * share, share), :],
-                dst_ref=chosen.at[k, :, pl.ds(r * share, share), :],
+                src_ref=chosen.at[k, :, pl.ds(PLACE[r] * share, share), :],
+                dst_ref=chosen.at[k, :, pl.ds(PLACE[r] * share, share), :],
                 send_sem=ch_send.at[r, k], recv_sem=ch_recv.at[r, k],
                 device_id=sibling, device_id_type=MESH).wait_recv()
     pltpu.make_async_remote_copy(
@@ -196,19 +199,22 @@
         send_sem=ch_send.at[0, other], recv_sem=ch_recv.at[0, other],
         device_id=sibling, device_id_type=MESH).wait_recv()
 
+    def error_of(zs, k):
+        predicted = sum(
+            lax.dot_general(
+                states[:, h * half:(h + 1) * half], held[h, zs, k],
+                (((1,), (1,)), ((), ())), preferred_element_type=jnp.float32)
+            for h in range(2))
+        difference = predicted - chosen[k, zs].astype(jnp.float32)
+        squares[...] += jnp.sum(difference * difference, axis=1, keepdims=True)
+        return difference.astype(jnp.bfloat16)
+
     def work(zs):
         for h in range(2):
             landed(h, zs, other)
 
         def one(k, carry):
-            predicted = sum(
-                lax.dot_general(
-                    states[:, h * half:(h + 1) * half], held[h, zs, k],
-                    (((1,), (1,)), ((), ())), preferred_element_type=jnp.float32)
-                for h in range(2))
-            difference = predicted - chosen[k, zs].astype(jnp.float32)
-            squares[...] += jnp.sum(difference * difference, axis=1, keepdims=True)
-            err = difference.astype(jnp.bfloat16)
+            err = error_of(zs, k)
             for h in range(2):
                 total[:, h * half:(h + 1) * half] += jnp.dot(
                     err, held[h, zs, k], preferred_element_type=jnp.float32)
@@ -216,60 +222,94 @@
 
         lax.fori_loop(0, CORES, one, 0)
 
+    last = jnp.where(z < LINE // 2, LINE - 1, 0)
+
     def round_of(distance, carry):
-        @pl.when(distance == LINE - 1)
-        def _():
-            arrive(LINE - 1)
-
-        @pl.when(z - distance >= 0)
+        @pl.when((z - distance >= 0) & (z - distance != last))
         def _():
             work(z - distance)
 
-        @pl.when((distance > 0) & (z + distance < LINE))
+        @pl.when((distance > 0) & (z + distance < LINE) & (z + distance != last))
         def _():
             work(z + distance)
 
         return carry
 
-    lax.fori_loop(0, LINE, round_of, 0)
+    lax.fori_loop(0, LINE - 1, round_of, 0)
+    arrive(LINE - 1)
+
+    errors[0] = error_of(last, core)
+    for h in range(2):
+        landed(h, last, other)
+    errors[1] = error_of(last, other)
+
+    def finish(first, count, h):
+        at = slice(first * share, (first + count) * share)
+        value = total[at, h * half:(h + 1) * half]
+        for i, k in enumerate((core, other)):
+            value += jnp.dot(errors[i, at, :], held[h, last, k], preferred_element_type=jnp.float32)
+        return value
+
+    sums = []
+
+    def send(source, dest, send_sem, recv_sem, target):
+        copy = pltpu.make_async_remote_copy(
+            src_ref=source, dst_ref=dest, send_sem=send_sem, recv_sem=recv_sem,
+            device_id=target, device_id_type=MESH)
+        copy.start()
+        sums.append(copy)
+        return copy
+
+    def send_half(h, part, target):
+        at = pl.ds(part * share, share)
+        return send(give.at[h, at, :], take.at[h, at, :], g_send.at[h, part], g_recv.at[h, part], target)
+
+    x_side, y_side = device(1, core), device(2, core)
+    give[0] = finish(2, 2, 0).astype(jnp.bfloat16)
+    x_mid, x_own = send_half(0, 0, x_side), send_half(0, 1, x_side)
+    give[1] = finish(1, 2, 1).astype(jnp.bfloat16)
+    y_mid, y_own = send_half(1, 1, y_side), send_half(1, 0, y_side)
+    low, high = slice(0, half), slice(half, feat_dim)
+    total[:2 * share, low] = finish(0, 2, 0)
+    total[3 * share:, high] = finish(3, 1, 1)
 
     def square_row(r):
-        column = jnp.broadcast_to(squares[r * share:(r + 1) * share, :], (share, 128))
+        at = slice(PLACE[r] * share, (PLACE[r] + 1) * share)
+        column = jnp.broadcast_to(squares[at, :], (share, share))
         return column.T[:8, :]
 
-    sums = []
-    for r in (3, 1, 2):
-        give[r - 1] = total[r * share:(r + 1) * share, :].astype(jnp.bfloat16)
-        copy = pltpu.make_async_remote_copy(
-            src_ref=give.at[r - 1], dst_ref=take.at[r - 1],
-            send_sem=g_send.at[r - 1], recv_sem=g_recv.at[r - 1],
-            device_id=device(r, core), device_id_type=MESH)
-        copy.start()
+    x_mid.wait_recv()
+    give_mid[0] = (total[share:2 * share, low] + take[0, :share, :].astype(jnp.float32)).astype(jnp.bfloat16)
+    mids = [send(give_mid.at[0], take_mid.at[0], m_send.at[0], m_recv.at[0], y_side)]
+    y_mid.wait_recv()
+    give_mid[1] = (total[3 * share:, high] + take[1, share:, :].astype(jnp.float32)).astype(jnp.bfloat16)
+    mids.append(send(give_mid.at[1], take_mid.at[1], m_send.at[1], m_recv.at[1], x_side))
+    total[:share, high] = finish(0, 1, 1)
+    squared = []
+    for r in range(1, PLANE):
         give_sq[r - 1] = square_row(r)
-        copy_sq = pltpu.make_async_remote_copy(
-            src_ref=give_sq.at[r - 1], dst_ref=take_sq.at[r - 1],
-            send_sem=q_send.at[r - 1], recv_sem=q_recv.at[r - 1],
-            device_id=device(r, core), device_id_type=MESH)
-        copy_sq.start()
-        sums += [copy, copy_sq]
-    for copy in sums:
+        squared.append(send(
+            give_sq.at[r - 1], take_sq.at[r - 1], q_send.at[r - 1], q_recv.at[r - 1], device(r, core)))
+    x_own.wait_recv()
+    y_own.wait_recv()
+    own_take = (take.at[0, pl.ds(share, share), :], take.at[1, pl.ds(0, share), :])
+    for h, at in enumerate((low, high)):
+        total[:share, at] += own_take[h][...].astype(jnp.float32)
+    for copy in squared + mids:
         copy.wait_recv()
 
-    own_weight = mask[pl.ds(pl.multiple_of(core * share, share), share), :].astype(jnp.float32)
-    for h in range(2):
-        at = slice(h * half, (h + 1) * half)
-        summed = total[:share, at]
-        for r in range(1, PLANE):
-            summed += take[r - 1, :, at].astype(jnp.float32)
-        done[h] = (own_weight * summed).astype(jnp.bfloat16)
+    weight_row = mask[pl.ds(core, 1), :].astype(jnp.float32)
+    weight = jnp.broadcast_to(weight_row, (share, share)).T[:, :1]
+    for h, at in enumerate((low, high)):
+        summed = total[:share, at] + take_mid[h].astype(jnp.float32)
+        done[h] = (weight * summed).astype(jnp.bfloat16)
     cross = pltpu.make_async_remote_copy(
         src_ref=done.at[other], dst_ref=crossed, send_sem=x_send, recv_sem=x_recv,
         device_id=sibling, device_id_type=MESH)
     cross.start()
     grad_out[pl.ds(pl.multiple_of(core * share, share), share), :] = done[core]
     all_squares = square_row(0) + take_sq[0] + take_sq[1] + take_sq[2]
-    weight_row = jnp.broadcast_to(own_weight, (share, 128)).T[:8, :]
-    loss_out[...] = (weight_row * all_squares / width)[:1, :]
+    loss_out[...] = weight_row * all_squares[:1, :] / width
     cross.wait_recv()
     grad_out[pl.ds(pl.multiple_of(other * share, share), share), :] = crossed[...]
 
@@ -305,25 +345,29 @@
             pltpu.VMEM((2, LINE, CORES, rows, half), bf16),
             pltpu.VMEM((PLANE * share, feat_dim), bf16),
             pltpu.VMEM(teacher.shape, bf16),
+            pltpu.VMEM((tok, share), jnp.int32),
             pltpu.VMEM((PLANE, LINE, tok, rows), bf16),
             pltpu.VMEM((CORES, LINE, PLANE * share, rows), bf16),
             pltpu.VMEM((PLANE * share, feat_dim), f32),
             pltpu.VMEM((PLANE * share, 1), f32),
-            pltpu.VMEM((PLANE - 1, share, feat_dim), bf16),
-            pltpu.VMEM((PLANE - 1, share, feat_dim), bf16),
+            pltpu.VMEM((CORES, PLANE * share, rows), bf16),
+            pltpu.VMEM((2, 2 * share, half), bf16),
+            pltpu.VMEM((2, 2 * share, half), bf16),
+            pltpu.VMEM((2, share, half), bf16),
+            pltpu.VMEM((2, share, half), bf16),
             pltpu.VMEM((PLANE - 1, 8, share), f32),
             pltpu.VMEM((PLANE - 1, 8, share), f32),
             pltpu.VMEM((2, share, half), bf16),
             pltpu.VMEM((share, half), bf16),
             dma((2, LINE, CORES)), dma((2, LINE)), dma((2, LINE)), dma((2, LINE)), dma((2,)),
             dma((PLANE,)), dma((PLANE,)), dma((3,)), dma((PLANE, CORES)), dma((PLANE, CORES)),
-            dma((PLANE - 1,)), dma((PLANE - 1,)), dma((PLANE - 1,)), dma((PLANE - 1,)),
+            dma((2, 2)), dma((2, 2)), dma((2,)), dma((2,)), dma((PLANE - 1,)), dma((PLANE - 1,)),
             dma(()), dma(()),
         ],
         compiler_params=pltpu.CompilerParams(
-            collective_id=0, has_side_effects=True, vmem_limit_bytes=48 * 1024 * 1024),
+            collective_id=0, has_side_effects=True, vmem_limit_bytes=60 * 1024 * 1024),
         cost_estimate=pl.CostEstimate(flops=flops, bytes_accessed=16 * 1024 * 1024, transcendentals=0),
-    )(student, projector, teacher, layer_index[:, None], valid_mask[:, None])
+    )(student, projector, teacher, layer_index.reshape(CORES, share), valid_mask.reshape(CORES, share))
     return grad, loss.reshape(share)
 
 

time: 116 us -> 107 us (0.922)
  Pallas kernels: 109 us -> 103 us
  local copies, waits for them, and re-layouts: 5.38 us -> 2.97 us
    pallas_call x1, Pallas kernels: 109 us -> 103 us  [fast_body(): pl.pallas_call(kernel, out_shape=(jax.ShapeDtypeStruct((tok, half), bf16)...]
    broadcast_in_dim x2 -> x0, local copies, waits for them, and re-layouts: 1.62 us -> none  [the longest x1 0.81 us: fast_body(): valid_mask[:, None]]
    unnamed x6 -> x2, local copies, waits for them, and re-layouts: 3.77 us -> 2.97 us
where the time goes in v2:
time: 107 us
  Pallas kernels  103 us (96%)
  local copies, waits for them, and re-layouts  2.97 us (3%)
    pallas_call x1, Pallas kernels, fast_body(): pl.pallas_call(kernel, out_shape=(jax.ShapeDtypeStruct((tok, half), bf16)...  103 us
    unnamed x2, local copies, waits for them, and re-layouts  2.97 us

profile of v2, /device:TPU:0, one launch (start us, length us, event | category | flops | bytes accessed | tf_op | source)
XLA Modules:
  0.0 106.5 jit_solution(151573973728205323)
XLA Ops:
  0.6 102.9 %shard_map.68 = (bf16[256,1024]{1,0:T(8,128)(2,1)}, f32[1,128]{1,0:T(1,128)}) custom-call(bf16[256,2048]{1,0:T(8,128)(2,1)} %student.1, bf16[1,264,2048]{2,1,0:T(8,128)(2,1)} %projector.1, bf16[2,256,4224]{2,1,0:T(8,128)(2,1)} %teacher.1, s32[2,128]{1,0:T(2,128)} %bitcast.3, s32[2,128]{1,0:T(2,128)} %bitcast.4), custom_call_target="tpu_custom_call" | custom-call | flops 8858370048 | bytes 16777216 | tf_op jit(solution)/shard_map/pallas_call | solution.py:335
  103.5 1.9 %copy.9 = bf16[256,1024]{1,0:T(8,128)(2,1)} copy(bf16[256,1024]{1,0:T(8,128)(2,1)} %get-tuple-element.8) | data formatting | bytes 1048576
  105.4 1.1 %copy.10 = f32[128]{0:T(128)} copy(f32[128]{0:T(128)} %bitcast.5) | data formatting | bytes 1024

commit v3 on v2

--- a/solution.py
+++ b/solution.py
@@ -35,13 +35,15 @@
 
 def kernel(
     student, projector, teacher, layer, mask, grad_out, loss_out,
-    held, states, layers, second, stage, chosen, total, squares, errors, give, take, give_mid, take_mid, give_sq, take_sq, done, crossed,
+    held, states, layers, second, stage, stage_rest, chosen, chosen_rest, total, squares, errors, early, give, take, give_mid, take_mid, give_sq, take_sq, done, crossed,
     arrived, up_sem, down_sem, over_sem, own_sem,
-    state_send, state_recv, load_sem, ch_send, ch_recv, g_send, g_recv, m_send, m_recv, q_send, q_recv, x_send, x_recv,
+    state_send, state_recv, load_sem, ch_send, ch_recv, rest_send, rest_recv, g_send, g_recv, m_send, m_recv, q_send, q_recv, x_send, x_recv,
 ):
     feat_dim = student.shape[1]
     half = feat_dim // 2
     rows = projector.shape[1]
+    whole = rows // 128 * 128
+    rest = rows - whole
     tok = student.shape[0]
     share = tok // CORES
     width = teacher.shape[2] * CORES
@@ -108,8 +110,10 @@
             src_ref=held.at[h, zs, k], dst_ref=held.at[h, zs, k], send_sem=over_sem.at[h, zs],
             recv_sem=arrived.at[h, zs, k], device_id=sibling, device_id_type=MESH).wait_recv()
 
-    for h in range(2):
+    def own_rows_out(h):
         pass_on(projector.at[0, :, pl.ds(h * half, half)], h, z, lambda copy: copy.start())
+
+    own_rows_out(0)
 
     state_copies = [
         pltpu.make_async_remote_copy(
@@ -131,6 +135,7 @@
         at = pl.multiple_of(i * step_rows, step_rows)
         mapped = second[pl.ds(at, step_rows), :1] == 1
         for target in range(PLANE):
+            rests = []
             for zs in range(LINE):
                 first_column = (zs * PLANE + target) * rows
                 base = first_column // 128 * 128
@@ -141,33 +146,48 @@
                 picked = jnp.where(mapped, b, a)
                 if shift:
                     picked = pltpu.roll(picked, span - shift, 1)
-                stage[target, zs, pl.ds(at, step_rows), :] = picked[:, :rows].astype(jnp.bfloat16)
+                stage[target, zs, pl.ds(at, step_rows), :] = picked[:, :whole].astype(jnp.bfloat16)
+                rests.append(picked[:, whole:rows])
+            rests.append(jnp.zeros((step_rows, 128 - LINE * rest), jnp.float32))
+            stage_rest[target, pl.ds(at, step_rows), :] = jnp.concatenate(rests, axis=1).astype(jnp.bfloat16)
         return carry
 
     lax.fori_loop(0, tok // step_rows, choose, 0)
+    own_rows_out(1)
 
     def chosen_copy(r, k):
-        return pltpu.make_async_remote_copy(
-            src_ref=stage.at[across(r), :, pl.ds(k * share, share), :],
-            dst_ref=chosen.at[core, :, pl.ds(PLACE[r] * share, share), :],
-            send_sem=ch_send.at[r, k], recv_sem=ch_recv.at[r, core],
-            device_id=device(r, k), device_id_type=MESH)
-
-    own_chosen = pltpu.make_async_copy(
-        stage.at[q, :, pl.ds(core * share, share), :],
-        chosen.at[core, :, pl.ds(0, share), :], load_sem.at[2])
-    own_chosen.start()
-    to_sibling = chosen_copy(0, other)
-    to_sibling.start()
-    chosen_copies = [chosen_copy(r, k) for r in range(1, PLANE) for k in range(CORES)]
-    for copy in chosen_copies:
+        mine, theirs = pl.ds(k * share, share), pl.ds(PLACE[r] * share, share)
+        return [
+            pltpu.make_async_remote_copy(
+                src_ref=stage.at[across(r), :, mine, :], dst_ref=chosen.at[core, :, theirs, :],
+                send_sem=ch_send.at[r, k], recv_sem=ch_recv.at[r, core],
+                device_id=device(r, k), device_id_type=MESH),
+            pltpu.make_async_remote_copy(
+                src_ref=stage_rest.at[across(r), mine, :], dst_ref=chosen_rest.at[core, theirs, :],
+                send_sem=rest_send.at[r, k], recv_sem=rest_recv.at[r, core],
+                device_id=device(r, k), device_id_type=MESH),
+        ]
+
+    own_chosen = [
+        pltpu.make_async_copy(
+            stage.at[q, :, pl.ds(core * share, share), :],
+            chosen.at[core, :, pl.ds(0, share), :], load_sem.at[2]),
+        pltpu.make_async_copy(
+            stage_rest.at[q, pl.ds(core * share, share), :],
+            chosen_rest.at[core, pl.ds(0, share), :], load_sem.at[3]),
+    ]
+    chosen_copies = chosen_copy(0, other)
+    for r in (3, 1, 2):
+        for k in range(CORES):
+            chosen_copies += chosen_copy(r, k)
+    for copy in own_chosen + chosen_copies:
         copy.start()
 
     total[...] = jnp.zeros_like(total)
     squares[...] = jnp.zeros_like(squares)
 
-    def arrive(distance):
-        for h in range(2):
+    def arrive(distance, halves=(0, 1)):
+        for h in halves:
             for sign in (-1, 1):
                 zs = z + sign * distance
 
@@ -181,31 +201,33 @@
     for copy in own_rows:
         copy.wait()
     own_state.wait()
-    own_chosen.wait()
+    for copy in own_chosen:
+        copy.wait()
     for copy in state_copies:
         copy.wait_recv()
-    for r in range(PLANE):
+
+    def chosen_landed(r, k):
+        at = pl.ds(PLACE[r] * share, share)
+        for buffer, send_sem, recv_sem in (
+                (chosen.at[k, :, at, :], ch_send, ch_recv), (chosen_rest.at[k, at, :], rest_send, rest_recv)):
+            pltpu.make_async_remote_copy(
+                src_ref=buffer, dst_ref=buffer, send_sem=send_sem.at[r, k], recv_sem=recv_sem.at[r, k],
+                device_id=sibling, device_id_type=MESH).wait_recv()
+
+    chosen_landed(0, other)
+    for r in range(1, PLANE):
         for k in range(CORES):
-            if r == 0:
-                continue
-            pltpu.make_async_remote_copy(
-                src_ref=chosen.at[k, :, pl.ds(PLACE[r] * share, share), :],
-                dst_ref=chosen.at[k, :, pl.ds(PLACE[r] * share, share), :],
-                send_sem=ch_send.at[r, k], recv_sem=ch_recv.at[r, k],
-                device_id=sibling, device_id_type=MESH).wait_recv()
-    pltpu.make_async_remote_copy(
-        src_ref=chosen.at[other, :, pl.ds(0, share), :],
-        dst_ref=chosen.at[other, :, pl.ds(0, share), :],
-        send_sem=ch_send.at[0, other], recv_sem=ch_recv.at[0, other],
-        device_id=sibling, device_id_type=MESH).wait_recv()
-
-    def error_of(zs, k):
-        predicted = sum(
-            lax.dot_general(
-                states[:, h * half:(h + 1) * half], held[h, zs, k],
-                (((1,), (1,)), ((), ())), preferred_element_type=jnp.float32)
-            for h in range(2))
-        difference = predicted - chosen[k, zs].astype(jnp.float32)
+            chosen_landed(r, k)
+
+    def project(zs, k, h):
+        return lax.dot_general(
+            states[:, h * half:(h + 1) * half], held[h, zs, k],
+            (((1,), (1,)), ((), ())), preferred_element_type=jnp.float32)
+
+    def error_of(zs, k, predicted):
+        side = pltpu.roll(chosen_rest[k].astype(jnp.float32), (LINE - zs) * rest + 128 - LINE * rest, 1)
+        targets = jnp.concatenate([chosen[k, zs].astype(jnp.float32), side[:, :rest]], axis=1)
+        difference = predicted - targets
         squares[...] += jnp.sum(difference * difference, axis=1, keepdims=True)
         return difference.astype(jnp.bfloat16)
 
@@ -214,7 +236,7 @@
             landed(h, zs, other)
 
         def one(k, carry):
-            err = error_of(zs, k)
+            err = error_of(zs, k, project(zs, k, 0) + project(zs, k, 1))
             for h in range(2):
                 total[:, h * half:(h + 1) * half] += jnp.dot(
                     err, held[h, zs, k], preferred_element_type=jnp.float32)
@@ -236,12 +258,15 @@
         return carry
 
     lax.fori_loop(0, LINE - 1, round_of, 0)
-    arrive(LINE - 1)
-
-    errors[0] = error_of(last, core)
-    for h in range(2):
-        landed(h, last, other)
-    errors[1] = error_of(last, other)
+    arrive(LINE - 1, (0,))
+
+    early[0] = project(last, core, 0)
+    landed(0, last, other)
+    early[1] = project(last, other, 0)
+    arrive(LINE - 1, (1,))
+    errors[0] = error_of(last, core, early[0] + project(last, core, 1))
+    landed(1, last, other)
+    errors[1] = error_of(last, other, early[1] + project(last, other, 1))
 
     def finish(first, count, h):
         at = slice(first * share, (first + count) * share)
@@ -265,12 +290,16 @@
         return send(give.at[h, at, :], take.at[h, at, :], g_send.at[h, part], g_recv.at[h, part], target)
 
     x_side, y_side = device(1, core), device(2, core)
-    give[0] = finish(2, 2, 0).astype(jnp.bfloat16)
-    x_mid, x_own = send_half(0, 0, x_side), send_half(0, 1, x_side)
-    give[1] = finish(1, 2, 1).astype(jnp.bfloat16)
-    y_mid, y_own = send_half(1, 1, y_side), send_half(1, 0, y_side)
     low, high = slice(0, half), slice(half, feat_dim)
+    give[0, :share, :] = finish(2, 1, 0).astype(jnp.bfloat16)
+    x_mid = send_half(0, 0, x_side)
+    give[1, share:, :] = finish(2, 1, 1).astype(jnp.bfloat16)
+    y_mid = send_half(1, 1, y_side)
     total[:2 * share, low] = finish(0, 2, 0)
+    give[0, share:, :] = finish(3, 1, 0).astype(jnp.bfloat16)
+    x_own = send_half(0, 1, x_side)
+    give[1, :share, :] = finish(1, 1, 1).astype(jnp.bfloat16)
+    y_own = send_half(1, 0, y_side)
     total[3 * share:, high] = finish(3, 1, 1)
 
     def square_row(r):
@@ -314,7 +343,7 @@
     grad_out[pl.ds(pl.multiple_of(other * share, share), share), :] = crossed[...]
 
     cross.wait_send()
-    for copy in sums + state_copies + chosen_copies + [to_sibling]:
+    for copy in sums + state_copies + chosen_copies:
         copy.wait_send()
 
     def sent(zs, carry):
@@ -328,7 +357,7 @@
 def fast_body(student, projector, teacher, layer_index, valid_mask):
     tok, feat_dim = student.shape
     rows = projector.shape[1]
-    half, share = feat_dim // 2, tok // CORES
+    half, share, whole = feat_dim // 2, tok // CORES, rows // 128 * 128
     bf16, f32 = jnp.bfloat16, jnp.float32
     dma = pltpu.SemaphoreType.DMA
     flops = 4 * tok * CORES * rows * LINE * CORES * feat_dim
@@ -346,11 +375,14 @@
             pltpu.VMEM((PLANE * share, feat_dim), bf16),
             pltpu.VMEM(teacher.shape, bf16),
             pltpu.VMEM((tok, share), jnp.int32),
-            pltpu.VMEM((PLANE, LINE, tok, rows), bf16),
-            pltpu.VMEM((CORES, LINE, PLANE * share, rows), bf16),
+            pltpu.VMEM((PLANE, LINE, tok, whole), bf16),
+            pltpu.VMEM((PLANE, tok, 128), bf16),
+            pltpu.VMEM((CORES, LINE, PLANE * share, whole), bf16),
+            pltpu.VMEM((CORES, PLANE * share, 128), bf16),
             pltpu.VMEM((PLANE * share, feat_dim), f32),
             pltpu.VMEM((PLANE * share, 1), f32),
             pltpu.VMEM((CORES, PLANE * share, rows), bf16),
+            pltpu.VMEM((CORES, PLANE * share, rows), f32),
             pltpu.VMEM((2, 2 * share, half), bf16),
             pltpu.VMEM((2, 2 * share, half), bf16),
             pltpu.VMEM((2, share, half), bf16),
@@ -360,7 +392,8 @@
             pltpu.VMEM((2, share, half), bf16),
             pltpu.VMEM((share, half), bf16),
             dma((2, LINE, CORES)), dma((2, LINE)), dma((2, LINE)), dma((2, LINE)), dma((2,)),
-            dma((PLANE,)), dma((PLANE,)), dma((3,)), dma((PLANE, CORES)), dma((PLANE, CORES)),
+            dma((PLANE,)), dma((PLANE,)), dma((4,)), dma((PLANE, CORES)), dma((PLANE, CORES)),
+            dma((PLANE, CORES)), dma((PLANE, CORES)),
             dma((2, 2)), dma((2, 2)), dma((2,)), dma((2,)), dma((PLANE - 1,)), dma((PLANE - 1,)),
             dma(()), dma(()),
         ],

time: 107 us -> 105 us (0.981)
  Pallas kernels: 103 us -> 101 us
    pallas_call x1, Pallas kernels: 103 us -> 101 us  [fast_body(): pl.pallas_call(kernel, out_shape=(jax.ShapeDtypeStruct((tok, half), bf16)...]
where the time goes in v3:
time: 105 us
  Pallas kernels  101 us (96%)
  local copies, waits for them, and re-layouts  2.97 us (3%)
    pallas_call x1, Pallas kernels, fast_body(): pl.pallas_call(kernel, out_shape=(jax.ShapeDtypeStruct((tok, half), bf16)...  101 us
    unnamed x2, local copies, waits for them, and re-layouts  2.97 us

profile of v3, /device:TPU:0, one launch (start us, length us, event | category | flops | bytes accessed | tf_op | source)
XLA Modules:
  0.0 105.1 jit_solution(5660284354979556541)
XLA Ops:
  0.6 101.4 %shard_map.68 = (bf16[256,1024]{1,0:T(8,128)(2,1)}, f32[1,128]{1,0:T(1,128)}) custom-call(bf16[256,2048]{1,0:T(8,128)(2,1)} %student.1, bf16[1,264,2048]{2,1,0:T(8,128)(2,1)} %projector.1, bf16[2,256,4224]{2,1,0:T(8,128)(2,1)} %teacher.1, s32[2,128]{1,0:T(2,128)} %bitcast.3, s32[2,128]{1,0:T(2,128)} %bitcast.4), custom_call_target="tpu_custom_call" | custom-call | flops 8858370048 | bytes 16777216 | tf_op jit(solution)/shard_map/pallas_call | solution.py:364
  102.1 1.9 %copy.9 = bf16[256,1024]{1,0:T(8,128)(2,1)} copy(bf16[256,1024]{1,0:T(8,128)(2,1)} %get-tuple-element.8) | data formatting | bytes 1048576
  104.0 1.1 %copy.10 = f32[128]{0:T(128)} copy(f32[128]{0:T(128)} %bitcast.5) | data formatting | bytes 1024
